TPU v7x, 32 devices: a whole 2x2x4 slice. The times are simulated.
32 devices in a mesh: gx: 2 (over y), gy: 16 (over z, x, core).
Axes of the slice: x: 2, y: 2, z: 4, core: 2. Of those that a mesh axis runs over, the one named last changes fastest.
Arguments:
- tokens: bfloat16 [4096, 768], P(('gx', 'gy')), may hold values from -6 to 6
- timesteps: int32 [64], P(('gx', 'gy')), may hold values from 0 to 999
- lengths: int32 [32, 2], P(('gx', 'gy')), may hold values from 1 to 96, 128 in all within a row
- routes: int32 [4096, 2], P(('gx', 'gy')), may hold values from 0 to 7, all different within a row; in each aligned block of 128 rows (0 to 127, 128 to 255, ...) at most 64 rows name the same one
- cotangent: bfloat16 [4096, 768], P(('gx', 'gy')), may hold values from -6 to 6
- w_ada: bfloat16 [768, 4608], P(('gx', 'gy')), may hold values from -0.625 to 0.625
- w_qkv: bfloat16 [768, 2304], P(('gx', 'gy')), may hold values from -0.21875 to 0.21875
- w_out: bfloat16 [768, 768], P(('gx', 'gy')), may hold values from -0.875 to 0.875
- w_fc1: bfloat16 [768, 3072], P(('gx', 'gy')), may hold values from -0.21875 to 0.21875
- w_fc2: bfloat16 [3072, 768], P(('gx', 'gy')), may hold values from -0.109375 to 0.109375
- w_router: bfloat16 [768, 8], P(('gx', 'gy')), may hold values from -0.15625 to 0.15625
- e_fc1: bfloat16 [8, 768, 3072], P('gx', 'gy'), may hold values from -0.21875 to 0.21875
- e_fc2: bfloat16 [8, 3072, 768], P('gx', 'gy'), may hold values from -0.4375 to 0.4375
Outputs:
- output: bfloat16 [4096, 768], P(('gx', 'gy'))
- d_tokens: float32 [4096, 768], P(('gx', 'gy'))
- d_w_ada: float32 [768, 4608], P(('gx', 'gy'))
- d_w_qkv: float32 [768, 2304], P(('gx', 'gy'))
- d_w_out: float32 [768, 768], P(('gx', 'gy'))
- d_w_fc1: float32 [768, 3072], P(('gx', 'gy'))
- d_w_fc2: float32 [3072, 768], P(('gx', 'gy'))
- d_w_router: float32 [768, 8], P(('gx', 'gy'))
- d_e_fc1: float32 [8, 768, 3072], P('gx', 'gy')
- d_e_fc2: float32 [8, 3072, 768], P('gx', 'gy')
Inputs may be any that keep to these rules, and one draw needn't show every extreme that they name: `lengths`: each device's row sums to 128; no item has more than 96 patches. `routes`: each row names two different experts. Among the rows of one device no expert is named more than 64 times; some device's rows name some expert exactly 64 times.
All inputs are finite; a program needn't handle non-finite values.
Results may differ from a plain program's by a relative error of at most 0.028.
Values may be sent and summed in bfloat16 or wider, within the bound.
A program may use at most 192 MiB of HBM per device.

v0:
```python
import math

import jax
import jax.numpy as jnp
from jax import lax
from jax.sharding import PartitionSpec as P

HEADS = 12
CAP = 64


precise = lax.Precision.HIGHEST
layer_epsilon = 1e-06


def layer_norm(values):
    average = jnp.mean(values, axis=-1, keepdims=True)
    centred = values - average
    return centred * lax.rsqrt(jnp.mean(centred * centred, axis=-1, keepdims=True) + layer_epsilon)


def modulate(values, shift_by, scale_by):
    return layer_norm(values) * (1.0 + scale_by) + shift_by


def sinusoid(timesteps, model_width):
    half_width = model_width // 2
    frequency = jnp.exp(-math.log(10000.0) * jnp.arange(half_width, dtype=jnp.float32) / half_width)
    angles = timesteps.astype(jnp.float32)[:, None] * frequency[None, :]
    return jnp.concatenate([jnp.cos(angles), jnp.sin(angles)], axis=1)


def membership(lengths, tok_count):
    bounds = jnp.cumsum(lengths)[:-1]
    position = jnp.arange(tok_count, dtype=jnp.int32)
    item_of = jnp.sum((position[:, None] >= bounds[None, :]).astype(jnp.int32), axis=1)
    item_ids = jnp.arange(lengths.shape[0], dtype=jnp.int32)
    return ((item_of[:, None] == item_ids[None, :]).astype(jnp.float32), item_of)


def slot_index(routes, expert_count, capacity):
    flat_routes = routes.reshape(-1)
    expert_hot = (
        flat_routes[:, None] == jnp.arange(expert_count, dtype=jnp.int32)[None, :]
    ).astype(jnp.int32)
    before = jnp.cumsum(expert_hot, axis=0) - expert_hot
    rank_in = jnp.sum(before * expert_hot, axis=1)
    return (flat_routes * capacity + rank_in).reshape(routes.shape)


def dot_float(left_side, right_side):
    return jnp.dot(left_side, right_side, preferred_element_type=jnp.float32)


def dot_rows(left_side, right_side):
    return jnp.einsum("td,tf->df", left_side, right_side, preferred_element_type=jnp.float32)


def dot_cols(left_side, right_side):
    return jnp.einsum("tf,df->td", left_side, right_side, preferred_element_type=jnp.float32)


def on_device(
    tokens,
    timesteps,
    lengths,
    routes,
    cotangent,
    w_ada,
    w_qkv,
    w_out,
    w_fc1,
    w_fc2,
    w_router,
    e_fc1,
    e_fc2,
):
    tok_count, model_width = tokens.shape
    head_count = HEADS
    head_size = model_width // head_count
    expert_count = w_router.shape[1]
    capacity = CAP
    score_scale = head_size ** (-0.5)
    residual = tokens.astype(jnp.float32)
    member, item_of = membership(lengths[0], tok_count)
    ada_full, qkv_full, out_full = (
        lax.all_gather(w_ada, ("gx", "gy"), axis=0, tiled=True),
        lax.all_gather(w_qkv, ("gx", "gy"), axis=0, tiled=True),
        lax.all_gather(w_out, ("gx", "gy"), axis=0, tiled=True),
    )
    condition = jax.nn.silu(sinusoid(timesteps, model_width)).astype(jnp.bfloat16)
    modulation = dot_float(condition, ada_full)
    token_mod = jnp.dot(member, modulation, precision=precise)
    shift_attn, scale_attn, gate_attn, shift_mlp, scale_mlp, gate_mlp = jnp.split(
        token_mod, 6, axis=1
    )
    attn_in = modulate(residual, shift_attn, scale_attn).astype(jnp.bfloat16)
    qkv_low = dot_float(attn_in, qkv_full).astype(jnp.bfloat16)
    queries, key_rows, value_rows = [
        portion.reshape(tok_count, head_count, head_size)
        for portion in jnp.split(qkv_low, 3, axis=1)
    ]
    same_item = item_of[:, None] == item_of[None, :]
    scores = (
        jnp.einsum("qhd,khd->hqk", queries, key_rows, preferred_element_type=jnp.float32)
        * score_scale
    )
    scores = jnp.where(same_item[None], scores, -1e30)
    attn_probs = jax.nn.softmax(scores, axis=-1)
    probs_low = attn_probs.astype(jnp.bfloat16)
    attn_low = jnp.einsum("hqk,khd->qhd", probs_low, value_rows, preferred_element_type=jnp.float32)
    attn_low = attn_low.reshape(tok_count, model_width).astype(jnp.bfloat16)
    attn_proj = dot_float(attn_low, out_full)
    middle = residual + gate_attn * attn_proj
    mixed_in = modulate(middle, shift_mlp, scale_mlp).astype(jnp.bfloat16)
    fc1_full, fc2_full, router_full = (
        lax.all_gather(w_fc1, ("gx", "gy"), axis=0, tiled=True),
        lax.all_gather(w_fc2, ("gx", "gy"), axis=0, tiled=True),
        lax.all_gather(w_router, ("gx", "gy"), axis=0, tiled=True),
    )
    hidden_pre = dot_float(mixed_in, fc1_full)
    hidden = jax.nn.gelu(hidden_pre).astype(jnp.bfloat16)
    shared = dot_float(hidden, fc2_full)
    chance = jax.nn.softmax(dot_float(mixed_in, router_full), axis=-1)
    expert_ids = jnp.arange(expert_count, dtype=jnp.int32)
    chosen = (routes[:, :, None] == expert_ids[None, None, :]).astype(jnp.float32)
    gate_values = jnp.sum(chosen * chance[:, None, :], axis=2)
    slot_of = slot_index(routes, expert_count, capacity)
    slot_ids = jnp.arange(expert_count * capacity, dtype=jnp.int32)
    selector = (slot_of[:, :, None] == slot_ids[None, None, :]).astype(jnp.bfloat16)
    slot_rows = jnp.einsum("tks,td->sd", selector, mixed_in, preferred_element_type=jnp.float32)
    slot_rows = slot_rows.astype(jnp.bfloat16).reshape(expert_count, capacity, model_width)
    owned_rows = lax.all_to_all(slot_rows, "gx", split_axis=0, concat_axis=1, tiled=True)
    expert_in, expert_back = (
        lax.all_gather(e_fc1, "gy", axis=1, tiled=True),
        lax.all_gather(e_fc2, "gy", axis=1, tiled=True),
    )
    inner_pre = jnp.einsum(
        "ecd,edf->ecf", owned_rows, expert_in, preferred_element_type=jnp.float32
    )
    inner_act = jax.nn.gelu(inner_pre).astype(jnp.bfloat16)
    result = jnp.einsum(
        "ecf,efd->ecd", inner_act, expert_back, preferred_element_type=jnp.float32
    ).astype(jnp.bfloat16)
    returned = lax.all_to_all(result, "gx", split_axis=1, concat_axis=0, tiled=True).reshape(
        expert_count * capacity, model_width
    )
    picked = jnp.take(returned, slot_of, axis=0).astype(jnp.float32)
    branch = shared + jnp.sum(gate_values[:, :, None] * picked, axis=1)
    output = (middle + gate_mlp * branch).astype(jnp.bfloat16)
    out_grad = cotangent.astype(jnp.float32)
    grad_gate_mlp = out_grad * branch
    grad_branch = out_grad * gate_mlp
    grad_shared = grad_branch.astype(jnp.bfloat16)
    grad_picked = (gate_values[:, :, None] * grad_branch[:, None, :]).astype(jnp.bfloat16)
    grad_gates = jnp.sum(grad_branch[:, None, :] * picked, axis=2)
    grad_slots = jnp.einsum(
        "tks,tkd->sd", selector, grad_picked, preferred_element_type=jnp.float32
    )
    grad_slots = grad_slots.astype(jnp.bfloat16).reshape(expert_count, capacity, model_width)
    grad_owned = lax.all_to_all(grad_slots, "gx", split_axis=0, concat_axis=1, tiled=True)
    grad_inner = jnp.einsum(
        "ecd,efd->ecf", grad_owned, expert_back, preferred_element_type=jnp.float32
    )
    unused_inner, gelu_expert = jax.vjp(jax.nn.gelu, inner_pre)
    grad_inner_pre = gelu_expert(grad_inner)[0].astype(jnp.bfloat16)
    term_e_out = jnp.einsum(
        "ecf,ecd->efd", inner_act, grad_owned, preferred_element_type=jnp.float32
    )
    term_e_in = jnp.einsum(
        "ecd,ecf->edf", owned_rows, grad_inner_pre, preferred_element_type=jnp.float32
    )
    grad_rows = jnp.einsum(
        "ecf,edf->ecd", grad_inner_pre, expert_in, preferred_element_type=jnp.float32
    )
    grad_returned = (
        lax.all_to_all(
            grad_rows.astype(jnp.bfloat16), "gx", split_axis=1, concat_axis=0, tiled=True
        )
        .astype(grad_rows.dtype)
        .reshape(expert_count * capacity, model_width)
    )
    sum_e_in, sum_e_out = (
        lax.psum_scatter(
            term_e_in.astype(jnp.bfloat16), "gy", scatter_dimension=1, tiled=True
        ).astype(jnp.float32),
        lax.psum_scatter(
            term_e_out.astype(jnp.bfloat16), "gy", scatter_dimension=1, tiled=True
        ).astype(jnp.float32),
    )
    grad_chance = jnp.sum(chosen * grad_gates[:, :, None], axis=1)
    grad_logits = chance * (grad_chance - jnp.sum(grad_chance * chance, axis=-1, keepdims=True))
    grad_logits = grad_logits.astype(jnp.bfloat16)
    grad_hidden = dot_cols(grad_shared, fc2_full)
    unused_shared, gelu_shared = jax.vjp(jax.nn.gelu, hidden_pre)
    grad_hidden_pre = gelu_shared(grad_hidden)[0].astype(jnp.bfloat16)
    term_fc2 = dot_rows(hidden, grad_shared)
    term_fc1 = dot_rows(mixed_in, grad_hidden_pre)
    term_router = dot_rows(mixed_in, grad_logits)
    part_fc1, part_fc2, part_router = (
        lax.psum_scatter(
            term_fc1.astype(jnp.bfloat16), "gx", scatter_dimension=0, tiled=True
        ).astype(jnp.float32),
        lax.psum_scatter(
            term_fc2.astype(jnp.bfloat16), "gx", scatter_dimension=0, tiled=True
        ).astype(jnp.float32),
        lax.psum_scatter(
            term_router.astype(jnp.bfloat16), "gx", scatter_dimension=0, tiled=True
        ).astype(jnp.float32),
    )
    sum_fc1, sum_fc2, sum_router = (
        lax.psum_scatter(
            part_fc1.astype(jnp.bfloat16), "gy", scatter_dimension=0, tiled=True
        ).astype(jnp.float32),
        lax.psum_scatter(
            part_fc2.astype(jnp.bfloat16), "gy", scatter_dimension=0, tiled=True
        ).astype(jnp.float32),
        lax.psum_scatter(
            part_router.astype(jnp.bfloat16), "gy", scatter_dimension=0, tiled=True
        ).astype(jnp.float32),
    )
    grad_mixed = dot_cols(grad_hidden_pre, fc1_full) + dot_cols(grad_logits, router_full)
    grad_mixed = grad_mixed + jnp.sum(jnp.take(grad_returned, slot_of, axis=0), axis=1)
    unused_mix, mix_back = jax.vjp(modulate, middle, shift_mlp, scale_mlp)
    grad_mid_norm, grad_shift_mlp, grad_scale_mlp = mix_back(grad_mixed)
    grad_middle = out_grad + grad_mid_norm
    grad_gate_attn = grad_middle * attn_proj
    grad_proj = (grad_middle * gate_attn).astype(jnp.bfloat16)
    term_out = dot_rows(attn_low, grad_proj)
    grad_attn = (
        dot_cols(grad_proj, out_full).astype(jnp.bfloat16).reshape(tok_count, head_count, head_size)
    )
    grad_probs = jnp.einsum(
        "qhd,khd->hqk", grad_attn, value_rows, preferred_element_type=jnp.float32
    )
    grad_values = jnp.einsum(
        "hqk,qhd->khd", probs_low, grad_attn, preferred_element_type=jnp.float32
    )
    grad_scores = attn_probs * (
        grad_probs - jnp.sum(grad_probs * attn_probs, axis=-1, keepdims=True)
    )
    grad_scores = grad_scores.astype(jnp.bfloat16)
    grad_queries = (
        jnp.einsum("hqk,khd->qhd", grad_scores, key_rows, preferred_element_type=jnp.float32)
        * score_scale
    )
    grad_keys = (
        jnp.einsum("hqk,qhd->khd", grad_scores, queries, preferred_element_type=jnp.float32)
        * score_scale
    )
    grad_qkv = jnp.concatenate(
        [
            grad_queries.reshape(tok_count, model_width),
            grad_keys.reshape(tok_count, model_width),
            grad_values.reshape(tok_count, model_width),
        ],
        axis=1,
    ).astype(jnp.bfloat16)
    term_qkv = dot_rows(attn_in, grad_qkv)
    grad_attn_in = dot_cols(grad_qkv, qkv_full)
    unused_pre, pre_back = jax.vjp(modulate, residual, shift_attn, scale_attn)
    grad_input_norm, grad_shift_attn, grad_scale_attn = pre_back(grad_attn_in)
    d_tokens = grad_middle + grad_input_norm
    grad_token_mod = jnp.concatenate(
        [
            grad_shift_attn,
            grad_scale_attn,
            grad_gate_attn,
            grad_shift_mlp,
            grad_scale_mlp,
            grad_gate_mlp,
        ],
        axis=1,
    )
    grad_modulation = jnp.einsum("ti,tc->ic", member, grad_token_mod, precision=precise).astype(
        jnp.bfloat16
    )
    all_condition, all_modgrad = (
        lax.all_gather(condition, ("gx", "gy"), axis=0, tiled=True),
        lax.all_gather(grad_modulation, ("gx", "gy"), axis=0, tiled=True),
    )
    own_share = model_width // lax.axis_size(("gx", "gy"))
    own_start = lax.axis_index(("gx", "gy")) * own_share
    own_condition = lax.dynamic_slice_in_dim(all_condition, own_start, own_share, 1)
    owned_ada = dot_rows(own_condition, all_modgrad)
    attn_terms = (term_qkv, term_out)
    attn_parts = (
        lax.psum_scatter(
            attn_terms[0].astype(jnp.bfloat16), "gx", scatter_dimension=0, tiled=True
        ).astype(jnp.float32),
        lax.psum_scatter(
            attn_terms[1].astype(jnp.bfloat16), "gx", scatter_dimension=0, tiled=True
        ).astype(jnp.float32),
    )
    attn_sums = (
        lax.psum_scatter(
            attn_parts[0].astype(jnp.bfloat16), "gy", scatter_dimension=0, tiled=True
        ).astype(jnp.float32),
        lax.psum_scatter(
            attn_parts[1].astype(jnp.bfloat16), "gy", scatter_dimension=0, tiled=True
        ).astype(jnp.float32),
    )
    sum_qkv, sum_out = attn_sums
    return (
        output,
        d_tokens,
        owned_ada,
        sum_qkv,
        sum_out,
        sum_fc1,
        sum_fc2,
        sum_router,
        sum_e_in,
        sum_e_out,
    )


def solution(mesh):
    in_specs = (
        P(("gx", "gy"), None),
        P(("gx", "gy")),
        P(("gx", "gy"), None),
        P(("gx", "gy"), None),
        P(("gx", "gy"), None),
        P(("gx", "gy"), None),
        P(("gx", "gy"), None),
        P(("gx", "gy"), None),
        P(("gx", "gy"), None),
        P(("gx", "gy"), None),
        P(("gx", "gy"), None),
        P("gx", "gy", None),
        P("gx", "gy", None),
    )
    out_specs = (
        P(("gx", "gy"), None),
        P(("gx", "gy"), None),
        P(("gx", "gy"), None),
        P(("gx", "gy"), None),
        P(("gx", "gy"), None),
        P(("gx", "gy"), None),
        P(("gx", "gy"), None),
        P(("gx", "gy"), None),
        P("gx", "gy", None),
        P("gx", "gy", None),
    )
    return jax.shard_map(
        on_device, mesh=mesh, in_specs=in_specs, out_specs=out_specs, check_vma=False
    )
```

profile of v0, /device:TPU:0, one launch (start us, length us, event | category | flops | bytes accessed | tf_op | source)
XLA Modules:
  0.0 1424.0 jit_solution(9216103235981631353)
XLA Ops:
  14.6 71.5 %all-gather.11.cloned.1.call-done = bf16[768,4608]{1,0:T(8,128)(2,1)} async-done(((bf16[24,4608]{1,0:T(8,128)(2,1)}), bf16[768,4608]{1,0:T(8,128)(2,1)}) %all-gather.11.cloned.1.call-update) | async-done | bytes 7077904 | tf_op jit(solution)/shard_map/all_gather | solution.py:87
  91.6 56.1 %all-gather.13.cloned.1.call-done = bf16[768,2304]{1,0:T(8,128)(2,1)} async-done(((bf16[24,2304]{1,0:T(8,128)(2,1)}), bf16[768,2304]{1,0:T(8,128)(2,1)}) %all-gather.13.cloned.1.call-update) | async-done | bytes 3538960 | tf_op jit(solution)/shard_map/all_gather | solution.py:88
  154.4 48.9 %all-gather.15.cloned.1.call-done = bf16[768,768]{1,0:T(8,128)(2,1)} async-done(((bf16[24,768]{1,0:T(8,128)(2,1)}), bf16[768,768]{1,0:T(8,128)(2,1)}) %all-gather.15.cloned.1.call-update) | async-done | bytes 1179664 | tf_op jit(solution)/shard_map/all_gather | solution.py:89
  207.2 61.4 %all-gather.17.cloned.1.call-done = bf16[768,3072]{1,0:T(8,128)(2,1)} async-done(((bf16[24,3072]{1,0:T(8,128)(2,1)}), bf16[768,3072]{1,0:T(8,128)(2,1)}) %all-gather.17.cloned.1.call-update) | async-done | bytes 4718608 | tf_op jit(solution)/shard_map/all_gather | solution.py:117
  271.8 62.0 %all-gather.19.cloned.1.call-done = bf16[3072,768]{1,0:T(8,128)(2,1)} async-done(((bf16[96,768]{1,0:T(8,128)(2,1)}), bf16[3072,768]{1,0:T(8,128)(2,1)}) %all-gather.19.cloned.1.call-update) | async-done | bytes 4718608 | tf_op jit(solution)/shard_map/all_gather | solution.py:118
  342.9 40.2 %all-gather = bf16[32,24,8]{1,2,0:T(8,128)(2,1)S(1)} all-gather(bf16[1,24,8]{1,2,0:T(8,128)(2,1)S(1)} %bitcast.144), channel_id=1, replica_groups=mesh['gx'=2,'gy'=16] {'gx','gy'}, dimensions={0}, use_global_device_ids=true | all-gather | bytes 12672 | tf_op jit(solution)/shard_map/all_gather | solution.py:119
  418.7 14.8 %all-gather.23.cloned.1.call-done = bf16[4,3072,768]{2,1,0:T(8,128)(2,1)} async-done(((bf16[4,192,768]{2,1,0:T(8,128)(2,1)}), bf16[4,3072,768]{2,1,0:T(8,128)(2,1)}) %all-gather.23.cloned.1.call-update) | async-done | bytes 18874384 | tf_op jit(solution)/shard_map/all_gather | solution.py:136
  433.5 11.5 fusion.82
  445.0 89.2 %all-gather.21.cloned.1.call-done = bf16[4,768,3072]{2,1,0:T(8,128)(2,1)} async-done(((bf16[4,48,3072]{2,1,0:T(8,128)(2,1)}), bf16[4,768,3072]{2,1,0:T(8,128)(2,1)}) %all-gather.21.cloned.1.call-update) | async-done | bytes 18874384 | tf_op jit(solution)/shard_map/all_gather | solution.py:135
  534.2 13.3 fusion.7
  547.5 11.3 convolution_convert_fusion.8
  564.0 11.9 convolution_convert_fusion.9
  590.9 17.2 %all-to-all-done.1 = bf16[4,128,768]{2,0,1:T(4,128)(2,1)S(1)} async-done(((bf16[4,128,768]{2,0,1:T(4,128)(2,1)}), bf16[4,128,768]{2,0,1:T(4,128)(2,1)S(1)}, u32[]{:S(2)}, u32[]{:S(2)}) %all-to-all-start.1) | async-done | bytes 786464 | tf_op jit(solution)/shard_map/all_to_all | solution.py:145
  640.4 35.4 %reduce-scatter.27.cloned.1.call-done = bf16[1536,768]{1,0:T(8,128)(2,1)} async-done(((bf16[3072,768]{1,0:T(8,128)(2,1)}), bf16[1536,768]{1,0:T(8,128)(2,1)}) %reduce-scatter.27.cloned.1.call-update) | async-done | bytes 2359312 | tf_op jit(solution)/shard_map/reduce_scatter | solution.py:204
  677.0 23.3 %reduce-scatter.19.cloned.1.call-done = bf16[384,768]{1,0:T(8,128)(2,1)} async-done(((bf16[768,768]{1,0:T(8,128)(2,1)}), bf16[384,768]{1,0:T(8,128)(2,1)}) %reduce-scatter.19.cloned.1.call-update) | async-done | bytes 589840 | tf_op jit(solution)/shard_map/reduce_scatter | solution.py:291
  700.3 50.0 %reduce-scatter.15.cloned.1.call-done = bf16[384,2304]{1,0:T(8,128)(2,1)} async-done(((bf16[768,2304]{1,0:T(8,128)(2,1)}), bf16[384,2304]{1,0:T(8,128)(2,1)}) %reduce-scatter.15.cloned.1.call-update) | async-done | bytes 1769488 | tf_op jit(solution)/shard_map/reduce_scatter | solution.py:288
  762.8 11.3 convolution_convert_fusion
  774.9 40.9 %all-gather.1 = bf16[32,2,768]{2,1,0:T(2,128)(2,1)S(1)} all-gather(bf16[1,2,768]{2,1,0:T(2,128)(2,1)S(1)} %fusion.71), channel_id=1, replica_groups=mesh['gx'=2,'gy'=16] {'gx','gy'}, dimensions={0}, use_global_device_ids=true | all-gather | bytes 101376 | tf_op jit(solution)/shard_map/all_gather | solution.py:279
  819.3 64.0 %reduce-scatter.29.cloned.1.call-done = bf16[96,768]{1,0:T(8,128)(2,1)} async-done(((bf16[1536,768]{1,0:T(8,128)(2,1)}), bf16[96,768]{1,0:T(8,128)(2,1)}) %reduce-scatter.29.cloned.1.call-update) | async-done | bytes 147472 | tf_op jit(solution)/shard_map/reduce_scatter | solution.py:215
  891.2 41.3 %all-gather.2 = bf16[32,2,4608]{2,1,0:T(2,128)(2,1)S(1)} all-gather(bf16[1,2,4608]{2,1,0:T(2,128)(2,1)S(1)} %fusion.8), channel_id=1, replica_groups=mesh['gx'=2,'gy'=16] {'gx','gy'}, dimensions={0}, use_global_device_ids=true | all-gather | bytes 608256 | tf_op jit(solution)/shard_map/all_gather | solution.py:280
  935.5 30.4 %all-reduce = bf16[384,8]{0,1:T(8,128)(2,1)S(1)} all-reduce(bf16[384,8]{0,1:T(8,128)(2,1)S(1)} %copy.153), channel_id=11, replica_groups=mesh['gx'=2,'gy'=16] {'gy'}, use_global_device_ids=true, to_apply=%region_33.34.clone | all-reduce | flops 3072 | bytes 12288
  968.0 49.1 %reduce-scatter.17.cloned.1.call-done = bf16[24,2304]{1,0:T(8,128)(2,1)} async-done(((bf16[384,2304]{1,0:T(8,128)(2,1)}), bf16[24,2304]{1,0:T(8,128)(2,1)}) %reduce-scatter.17.cloned.1.call-update) | async-done | bytes 110608 | tf_op jit(solution)/shard_map/reduce_scatter | solution.py:296
  1018.7 196.7 %reduce-scatter.31.cloned.1.call-done = bf16[4,48,3072]{2,1,0:T(8,128)(2,1)} async-done(((bf16[4,768,3072]{2,1,0:T(8,128)(2,1)}), bf16[4,48,3072]{2,1,0:T(8,128)(2,1)}) %reduce-scatter.31.cloned.1.call-update) | async-done | bytes 1179664 | tf_op jit(solution)/shard_map/reduce_scatter | solution.py:184
  1218.3 195.5 %reduce-scatter.33.cloned.1.call-done = bf16[4,192,768]{2,1,0:T(8,128)(2,1)} async-done(((bf16[4,3072,768]{2,1,0:T(8,128)(2,1)}), bf16[4,192,768]{2,1,0:T(8,128)(2,1)}) %reduce-scatter.33.cloned.1.call-update) | async-done | bytes 1179664 | tf_op jit(solution)/shard_map/reduce_scatter | solution.py:187
  (307 shorter events, 160.2 us)
Async XLA Ops:
  7.2 79.0 %all-gather.11.cloned.1.call-start = ((), (), s32[]{:S(2)}) async-start(), calls=%async_computation.15 | async-start | bytes 7299072 | tf_op jit(solution)/shard_map/all_gather | solution.py:87
  7.9 139.7 %all-gather.13.cloned.1.call-start = ((), (), s32[]{:S(2)}) async-start(), calls=%async_computation.16 | async-start | bytes 3649536 | tf_op jit(solution)/shard_map/all_gather | solution.py:88
  8.7 194.7 %all-gather.15.cloned.1.call-start = ((), (), s32[]{:S(2)}) async-start(), calls=%async_computation.17 | async-start | bytes 1216512 | tf_op jit(solution)/shard_map/all_gather | solution.py:89
  9.4 259.2 %all-gather.17.cloned.1.call-start = ((), (), s32[]{:S(2)}) async-start(), calls=%async_computation.18 | async-start | bytes 4866048 | tf_op jit(solution)/shard_map/all_gather | solution.py:117
  10.0 323.8 %all-gather.19.cloned.1.call-start = ((), (), s32[]{:S(2)}) async-start(), calls=%async_computation.19 | async-start | bytes 4866048 | tf_op jit(solution)/shard_map/all_gather | solution.py:118
  10.6 422.9 %all-gather.23.cloned.1.call-start = ((), (), s32[]{:S(2)}) async-start(), calls=%async_computation.21 | async-start | bytes 20054016 | tf_op jit(solution)/shard_map/all_gather | solution.py:136
  11.1 523.0 %all-gather.21.cloned.1.call-start = ((), (), s32[]{:S(2)}) async-start(), calls=%async_computation.20 | async-start | bytes 20054016 | tf_op jit(solution)/shard_map/all_gather | solution.py:135
  11.9 628.0 %reduce-scatter.23.cloned.1.call-start = ((), (), s32[]{:S(2)}) async-start(), calls=%async_computation.26 | async-start | bytes 7077888 | tf_op jit(solution)/shard_map/reduce_scatter | solution.py:201
  207.2 183.5 %copy-start.5 = (bf16[128,768]{1,0:T(8,128)(2,1)}, bf16[128,768]{1,0:T(8,128)(2,1)S(1)}, u32[]{:S(2)}) copy-start(bf16[128,768]{1,0:T(8,128)(2,1)S(1)} %get-tuple-element.22) | copy-start | bytes 589828
  207.2 199.5 %copy-start.9 = (f32[128,768]{1,0:T(8,128)}, f32[128,768]{1,0:T(8,128)S(1)}, u32[]{:S(2)}) copy-start(f32[128,768]{1,0:T(8,128)S(1)} %get-tuple-element.23) | copy-start | bytes 1179652
  387.0 15.1 %all-to-all-start.2 = ((bf16[8,64,768]{2,1,0:T(8,128)(2,1)}), bf16[8,64,768]{2,1,0:T(8,128)(2,1)S(1)}, u32[]{:S(2)}, u32[]{:S(2)}) async-start(bf16[8,64,768]{2,1,0:T(8,128)(2,1)} %bitcast.122), calls=%async_computation.2 | async-start | bytes 1572864 | tf_op jit(solution)/shard_map/all_to_all | solution.py:161
  402.1 15.3 %all-to-all-start = ((bf16[8,64,768]{2,1,0:T(8,128)(2,1)}), bf16[8,64,768]{2,1,0:T(8,128)(2,1)}, u32[]{:S(2)}, u32[]{:S(2)}) async-start(bf16[8,64,768]{2,1,0:T(8,128)(2,1)} %bitcast.121), calls=%async_computation | async-start | bytes 1572864 | tf_op jit(solution)/shard_map/all_to_all | solution.py:133
  406.5 269.3 %reduce-scatter.27.cloned.1.call-start = ((), (), s32[]{:S(2)}) async-start(), calls=%async_computation.28 | async-start | bytes 7077888 | tf_op jit(solution)/shard_map/reduce_scatter | solution.py:204
  560.3 24.1 %all-to-all-start.3 = ((bf16[4,128,768]{2,0,1:T(4,128)(2,1)}), bf16[4,128,768]{2,0,1:T(4,128)(2,1)S(1)}, u32[]{:S(2)}, u32[]{:S(2)}) async-start(bf16[4,128,768]{2,0,1:T(4,128)(2,1)} %copy.137), calls=%async_computation.3 | async-start | bytes 1572864 | tf_op jit(solution)/shard_map/all_to_all | solution.py:177
  584.4 23.7 %all-to-all-start.1 = ((bf16[4,128,768]{2,0,1:T(4,128)(2,1)}), bf16[4,128,768]{2,0,1:T(4,128)(2,1)S(1)}, u32[]{:S(2)}, u32[]{:S(2)}) async-start(bf16[4,128,768]{2,0,1:T(4,128)(2,1)} %copy.132), calls=%async_computation.1 | async-start | bytes 1572864 | tf_op jit(solution)/shard_map/all_to_all | solution.py:145
  588.0 112.3 %reduce-scatter.19.cloned.1.call-start = ((), (), s32[]{:S(2)}) async-start(), calls=%async_computation.24 | async-start | bytes 1769472 | tf_op jit(solution)/shard_map/reduce_scatter | solution.py:291
  628.8 121.5 %reduce-scatter.15.cloned.1.call-start = ((), (), s32[]{:S(2)}) async-start(), calls=%async_computation.22 | async-start | bytes 5308416 | tf_op jit(solution)/shard_map/reduce_scatter | solution.py:288
  639.8 177.9 %reduce-scatter.25.cloned.1.call-start = ((), (), s32[]{:S(2)}) async-start(), calls=%async_computation.27 | async-start | bytes 2506752 | tf_op jit(solution)/shard_map/reduce_scatter | solution.py:212
  640.4 243.0 %reduce-scatter.29.cloned.1.call-start = ((), (), s32[]{:S(2)}) async-start(), calls=%async_computation.29 | async-start | bytes 2506752 | tf_op jit(solution)/shard_map/reduce_scatter | solution.py:215
  675.8 258.7 %reduce-scatter.35.cloned.1.call-start = ((), (), s32[]{:S(2)}) async-start(), calls=%async_computation.32 | async-start | bytes 294912
  676.9 289.7 %reduce-scatter.21.cloned.1.call-start = ((), (), s32[]{:S(2)}) async-start(), calls=%async_computation.25 | async-start | bytes 626688 | tf_op jit(solution)/shard_map/reduce_scatter | solution.py:299
  700.3 316.8 %reduce-scatter.17.cloned.1.call-start = ((), (), s32[]{:S(2)}) async-start(), calls=%async_computation.23 | async-start | bytes 1880064 | tf_op jit(solution)/shard_map/reduce_scatter | solution.py:296
  750.3 465.1 %reduce-scatter.31.cloned.1.call-start = ((), (), s32[]{:S(2)}) async-start(), calls=%async_computation.30 | async-start | bytes 20054016 | tf_op jit(solution)/shard_map/reduce_scatter | solution.py:184
  761.7 652.1 %reduce-scatter.33.cloned.1.call-start = ((), (), s32[]{:S(2)}) async-start(), calls=%async_computation.31 | async-start | bytes 20054016 | tf_op jit(solution)/shard_map/reduce_scatter | solution.py:187
  (74 other events, 2203.1 us)
Sparse Core Ops, SparseCore 0:
  10.9 75.2 all-gather.10
  89.0 58.5 all-gather.12
  150.5 52.7 all-gather.14
  206.1 62.5 all-gather.16
  271.4 62.3 all-gather.18
  335.2 98.2 all-gather.22
  435.0 99.1 all-gather.20
  536.5 76.8 reduce-scatter.22
  615.8 60.0 reduce-scatter.26
  678.5 21.7 reduce-scatter.18
  702.6 47.6 reduce-scatter.14
  753.9 63.1 reduce-scatter.24
  821.4 61.9 reduce-scatter.28
  885.4 9.9 reduce-scatter.34
  898.9 54.8 reduce-scatter.20
  957.8 59.2 reduce-scatter.16
  1021.6 193.7 reduce-scatter.30
  1219.9 193.8 reduce-scatter.32
where the time goes:
time: 1430 us; the launch traced here: 1420 us
  waiting for transfers between devices  1060 us (74%)
  blocking collectives  153 us (11%)
  matrix products  128 us (9%)
  local copies, waits for them, and re-layouts  24.5 us (2%)
  other arithmetic  22.2 us (2%)
  between operations  16.5 us (1%)
  starting transfers between devices  16.3 us (1%)
    reduce_scatter x1, waiting for transfers between devices, on_device(): lax.psum_scatter(term_e_in.astype(jnp.bfloat16), 'gy', scatter_dimension=...  197 us
    reduce_scatter x1, waiting for transfers between devices, on_device(): lax.psum_scatter(term_e_out.astype(jnp.bfloat16), 'gy', scatter_dimension...  195 us
    all_gather x1, waiting for transfers between devices, on_device(): lax.all_gather(e_fc1, 'gy', axis=1, tiled=True)  89.2 us
    all_gather x1, waiting for transfers between devices, on_device(): lax.all_gather(w_ada, ('gx', 'gy'), axis=0, tiled=True)  71.5 us
    reduce_scatter x1, waiting for transfers between devices, on_device(): lax.psum_scatter(part_fc2.astype(jnp.bfloat16), 'gy', scatter_dimension=0...  64 us
    all_gather x1, waiting for transfers between devices, on_device(): lax.all_gather(w_fc2, ('gx', 'gy'), axis=0, tiled=True)  62 us
    all_gather x1, waiting for transfers between devices, on_device(): lax.all_gather(w_fc1, ('gx', 'gy'), axis=0, tiled=True)  61.4 us
    all_gather x1, waiting for transfers between devices, on_device(): lax.all_gather(w_qkv, ('gx', 'gy'), axis=0, tiled=True)  56.1 us
  transfers between devices with their start and end apart: 22, of which 18 were waited for; matrix products, arithmetic and copies ran while one was open for 12% of the time, Pallas kernels for 0%

commit v1 on v0

--- a/solution.py
+++ b/solution.py
@@ -1,16 +1,701 @@
+import functools
 import math
 
 import jax
 import jax.numpy as jnp
 from jax import lax
+from jax.experimental import pallas as pl
+from jax.experimental.pallas import tpu as pltpu
 from jax.sharding import PartitionSpec as P
 
 HEADS = 12
 CAP = 64
-
+MESH = pl.DeviceIdType.MESH
+ANY = pl.ANY
+VMEM = pltpu.VMEM
+DMA = pltpu.SemaphoreType.DMA
+LINE = (1, 3, 2)
 
 precise = lax.Precision.HIGHEST
 layer_epsilon = 1e-06
+
+
+def place():
+    gy = lax.axis_index("gy")
+    return lax.axis_index("gx"), gy // 4, (gy // 2) % 2, gy % 2
+
+
+def device(y, z, x, c):
+    return (y, 4 * z + 2 * x + c)
+
+
+def chip(y, z, x):
+    return 8 * y + 2 * z + x
+
+
+def meet(partners):
+    barrier = pltpu.get_barrier_semaphore()
+    for partner in partners:
+        pl.semaphore_signal(barrier, inc=1, device_id=partner, device_id_type=MESH)
+    pl.semaphore_wait(barrier, len(partners))
+
+
+def cross_partners(here):
+    y, z, x, c = here
+    return [device(y, (z + step) % 4, x, c) for step in LINE] + [
+        device(1 - y, z, x, c),
+        device(y, z, 1 - x, c),
+    ]
+
+
+def remote(source, target, send, recv, to):
+    return pltpu.make_async_remote_copy(
+        src_ref=source, dst_ref=target, send_sem=send, recv_sem=recv, device_id=to, device_id_type=MESH
+    )
+
+
+class Gather:
+    def __init__(self, here, y_first, own, slot, send, recv, pair=None):
+        self.here, self.y_first, self.own, self.slot = here, y_first, own, slot
+        self.send, self.recv, self.pair, self.started = send, recv, pair, []
+
+    def copy(self, source, number, recv, to):
+        sent = remote(source, self.slot(number), self.send.at[len(self.started)], recv.at[number], to)
+        sent.start()
+        self.started.append(sent)
+
+    def forward(self, source, number, to_y, to_x):
+        y, z, x, c = self.here
+        if to_y:
+            self.copy(source, number, self.recv, device(1 - y, z, x, c))
+        if to_x:
+            self.copy(source, number, self.recv, device(y, z, 1 - x, c))
+        if self.pair is not None:
+            self.copy(source, number, self.pair, device(y, z, x, 1 - c))
+
+    def arrive(self, number, recv=None):
+        recv = self.recv if recv is None else recv
+        block = self.slot(number)
+        remote(block, block, self.send.at[0], recv.at[number], device(*self.here)).wait_recv()
+        return block
+
+    def start(self):
+        y, z, x, c = self.here
+        number = chip(y, z, x)
+        for step in LINE:
+            self.copy(self.own, number, self.recv, device(y, (z + step) % 4, x, c))
+        self.forward(self.own, number, True, True)
+
+    def line(self, step):
+        y, z, x, c = self.here
+        number = chip(y, (z + step) % 4, x)
+        self.forward(self.arrive(number), number, True, True)
+
+    def second(self, step):
+        y, z, x, c = self.here
+        if self.y_first:
+            number = chip(1 - y, (z + step) % 4, x)
+        else:
+            number = chip(y, (z + step) % 4, 1 - x)
+        self.forward(self.arrive(number), number, not self.y_first, self.y_first)
+
+    def third(self, step):
+        y, z, x, c = self.here
+        for other in (0, 1):
+            if self.y_first:
+                number = chip(y if other == 0 else 1 - y, (z + step) % 4, 1 - x)
+            else:
+                number = chip(1 - y, (z + step) % 4, x if other == 0 else 1 - x)
+            self.forward(self.arrive(number), number, False, False)
+
+    def finish(self):
+        for sent in self.started:
+            sent.wait_send()
+        if self.pair is not None:
+            for number in range(16):
+                self.arrive(number, self.pair)
+
+
+def gather_all(gathers, between=None):
+    for gather in gathers:
+        gather.start()
+    for gather in gathers:
+        gather.second(0)
+    for step in LINE:
+        for gather in gathers:
+            gather.line(step)
+        for gather in gathers:
+            gather.second(step)
+    if between is not None:
+        between()
+    for step in (0,) + LINE:
+        for gather in gathers:
+            gather.third(step)
+    for gather in gathers:
+        gather.finish()
+
+
+class Scatter:
+    def __init__(self, here, y_first, part, got, send, recv):
+        self.here, self.y_first, self.part, self.got = here, y_first, part, got
+        self.send, self.recv, self.started = send, recv, []
+
+    def number(self, a, b, step):
+        y, z, x, c = self.here
+        flip_y, flip_x = (a, b) if self.y_first else (b, a)
+        return chip(1 - y if flip_y else y, (z + step) % 4, 1 - x if flip_x else x)
+
+    def toward(self, second):
+        y, z, x, c = self.here
+        return device(1 - y, z, x, c) if self.y_first != second else device(y, z, 1 - x, c)
+
+    def copy(self, source, index, to):
+        sent = remote(source, self.got(index), self.send.at[len(self.started)], self.recv.at[index], to)
+        sent.start()
+        self.started.append(sent)
+
+    def arrive(self, index):
+        block = self.got(index)
+        remote(block, block, self.send.at[0], self.recv.at[index], device(*self.here)).wait_recv()
+        return block
+
+    def first(self, step):
+        for b in (1, 0):
+            self.copy(self.part(self.number(1, b, step)), 4 * b + step, self.toward(False))
+
+    def add(self, number, index):
+        block, mine = self.arrive(index), self.part(number)
+        total = mine[...].astype(jnp.float32) + block[...].astype(jnp.float32)
+        mine[...] = total.astype(mine.dtype)
+
+    def one(self, b, step):
+        number = self.number(0, b, step)
+        self.add(number, 4 * b + step)
+        if b == 1:
+            self.copy(self.part(number), 8 + step, self.toward(True))
+
+    def two(self, step):
+        y, z, x, c = self.here
+        number = self.number(0, 0, step)
+        self.add(number, 8 + step)
+        if step:
+            self.copy(self.part(number), 11 + step, device(y, (z + step) % 4, x, c))
+
+    def total(self):
+        result = self.part(self.number(0, 0, 0))[...].astype(jnp.float32)
+        for step in (1, 2, 3):
+            result = result + self.arrive(11 + step)[...].astype(jnp.float32)
+        return result
+
+    def finish(self):
+        for sent in self.started:
+            sent.wait_send()
+
+
+def scatter_all(scatters):
+    order = (2, 1, 3, 0)
+    for scatter in scatters:
+        scatter.first(order[0])
+    for scatter in scatters:
+        scatter.first(order[1])
+    for turn, step in enumerate(order):
+        for scatter in scatters:
+            scatter.one(1, step)
+        for scatter in scatters:
+            scatter.one(0, step)
+        if turn + 2 < 4:
+            for scatter in scatters:
+                scatter.first(order[turn + 2])
+        for scatter in scatters:
+            scatter.two(step)
+
+
+def weights_kernel(
+    fold, e1, e2, f1, f2, ada, qkv, out, w1, w1s, w2, w2s, stage, block_a, block_q, block_o,
+    pre_send, pre_recv, g_send, g_recv, g_pair, a_send, a_recv, a_pair_send, a_pair, b_send, b_recv, b_pair, l_sem, d_send, d_recv,
+):
+    here = y, z, x, c = place()
+    me, k, gy = chip(y, z, x), 2 * z + x, 4 * z + 2 * x + c
+    rows = fold.shape[1]
+    others = [(dy, dz, dx) for dy in (0, 1) for dz in (0, 1, 2, 3) for dx in (0, 1) if (dy, dz, dx) != (0, 0, 0)]
+    spot = lambda dy, dz, dx: (1 - y if dy else y, (z + dz) % 4, 1 - x if dx else x)
+    sibling = device(y, z, x, 1 - c)
+    meet([device(*spot(*o), c) for o in others] + [sibling])
+
+    pre = remote(fold.at[1 - c], stage.at[pl.ds(pl.multiple_of(rows * c, 8), rows)], pre_send, pre_recv, sibling)
+    pre.start()
+    stage[pl.ds(pl.multiple_of(rows * c, 8), rows), :] = fold[c]
+
+    depth = e1.shape[1]
+    width = w1.shape[2]
+    cols = lambda n: pl.ds(pl.multiple_of(width * n, 128), width)
+    strip = lambda n: pl.ds(pl.multiple_of(depth * n, 16), depth)
+    started = []
+    plane = [o for o in others if o[0] == 0]
+    local = [
+        pltpu.make_async_copy(e1.at[:, :, cols(k)], w1.at[:, strip(gy), :], l_sem.at[0]),
+        pltpu.make_async_copy(e2, w2.at[:, pl.ds(pl.multiple_of(e2.shape[1] * c, 16), e2.shape[1]), :], l_sem.at[1]),
+        pltpu.make_async_copy(f2, w2s.at[pl.ds(pl.multiple_of(f2.shape[0] * c, 16), f2.shape[0]), :], l_sem.at[2]),
+        pltpu.make_async_copy(f1.at[me], w1s.at[c, me], l_sem.at[3]),
+    ]
+    for copy in local:
+        copy.start()
+    for i, o in enumerate(plane):
+        ty, tz, tx = spot(*o)
+        copy = remote(
+            e1.at[:, :, cols(2 * tz + tx)], w1.at[:, strip(gy), :], a_send.at[i], a_recv.at[k], device(ty, tz, tx, c)
+        )
+        copy.start()
+        started.append(copy)
+    for i, o in enumerate(others):
+        ty, tz, tx = spot(*o)
+        copy = remote(f1.at[chip(ty, tz, tx)], w1s.at[c, me], b_send.at[i], b_recv.at[me], device(ty, tz, tx, c))
+        copy.start()
+        started.append(copy)
+    twin = [
+        remote(e2, w2.at[:, pl.ds(pl.multiple_of(e2.shape[1] * c, 16), e2.shape[1]), :], d_send.at[0], d_recv.at[0], sibling),
+        remote(f2, w2s.at[pl.ds(pl.multiple_of(f2.shape[0] * c, 16), f2.shape[0]), :], d_send.at[1], d_recv.at[1], sibling),
+    ]
+    for copy in twin:
+        copy.start()
+
+    pre.wait()
+    at = 0
+    for block in (block_a, block_q, block_o):
+        block[...] = stage[:, at : at + block.shape[1]].astype(jnp.bfloat16)
+        at += block.shape[1]
+    gathers, own = [], []
+    for i, (block, full, y_first) in enumerate(((block_a, ada, True), (block_q, qkv, False), (block_o, out, False))):
+        slot = functools.partial(lambda full, n: full.at[c, pl.ds(pl.multiple_of(2 * rows * n, 16), 2 * rows), :], full)
+        gathers.append(Gather(here, y_first, block, slot, g_send.at[i], g_recv.at[i], g_pair.at[i]))
+        copy = pltpu.make_async_copy(block, slot(me), l_sem.at[4 + i])
+        copy.start()
+        own.append(copy)
+
+    def pass_on():
+        for copy in local:
+            copy.wait()
+        for i, (dz, dx) in enumerate([(0, 0)] + [(o[1], o[2]) for o in plane]):
+            sy, sz, sx = spot(0, dz, dx)
+            source = 2 * sz + sx
+            block = w1.at[:, strip(2 * source + c), :]
+            if i:
+                remote(block, block, a_send.at[0], a_recv.at[source], sibling).wait_recv()
+            copy = remote(block, block, a_pair_send.at[i], a_pair.at[source], sibling)
+            copy.start()
+            started.append(copy)
+        for o in others:
+            number = chip(*spot(*o))
+            remote(w1s.at[c, number], w1s.at[c, number], b_send.at[0], b_recv.at[number], sibling).wait_recv()
+        copy = remote(w1s.at[c], w1s.at[c], b_pair.at[0], b_pair.at[1], sibling)
+        copy.start()
+        started.append(copy)
+
+    gather_all(gathers, pass_on)
+    for copy in own:
+        copy.wait()
+    for copy in started:
+        copy.wait_send()
+    for source in range(8):
+        block = w1.at[:, strip(2 * source + 1 - c), :]
+        remote(block, block, a_send.at[0], a_pair.at[source], sibling).wait_recv()
+    remote(w1s.at[1 - c], w1s.at[1 - c], b_pair.at[0], b_pair.at[1], sibling).wait_recv()
+    for copy in twin:
+        copy.wait_send()
+    other = pl.ds(pl.multiple_of(e2.shape[1] * (1 - c), 16), e2.shape[1])
+    remote(w2.at[:, other, :], w2.at[:, other, :], d_send.at[0], d_recv.at[0], sibling).wait_recv()
+    other = pl.ds(pl.multiple_of(f2.shape[0] * (1 - c), 16), f2.shape[0])
+    remote(w2s.at[other, :], w2s.at[other, :], d_send.at[1], d_recv.at[1], sibling).wait_recv()
+
+
+def gather_weights(w_ada, w_qkv, w_out, w_fc1, w_fc2, e_fc1, e_fc2):
+    rows, model = w_out.shape
+    half = lambda w, c: w[:, c * (w.shape[1] // 2) : (c + 1) * (w.shape[1] // 2)]
+    fold = jnp.stack([jnp.concatenate([half(w, c) for w in (w_ada, w_qkv, w_out)], axis=1) for c in (0, 1)])
+    fold = fold.astype(jnp.float32)
+    ff = w_fc1.shape[1]
+    slim = ff // 16
+    f1 = w_fc1.reshape(rows, 16, slim).transpose(1, 0, 2).reshape(16, rows // 2, 2 * slim)
+    f1 = jnp.pad(f1, ((0, 0), (0, 16 - rows // 2), (0, 0)))
+    experts, depth, _ = e_fc1.shape
+    wide = ff // 8
+    bf = jnp.bfloat16
+    shape = jax.ShapeDtypeStruct
+    out_shape = (
+        shape((2, model, w_ada.shape[1] // 2), bf),
+        shape((2, model, w_qkv.shape[1] // 2), bf),
+        shape((2, model, w_out.shape[1] // 2), bf),
+        shape((experts, model, wide), bf),
+        shape((2, 16, 16, 2 * slim), bf),
+        shape((experts, 2 * e_fc2.shape[1], model), bf),
+        shape((2 * w_fc2.shape[0], model), bf),
+    )
+    ada, qkv, out, w1, w1s, w2, w2s = pl.pallas_call(
+        weights_kernel,
+        out_shape=out_shape,
+        in_specs=[pl.BlockSpec(memory_space=VMEM)] + [pl.BlockSpec(memory_space=ANY)] * 4,
+        out_specs=[pl.BlockSpec(memory_space=ANY)] * 7,
+        scratch_shapes=[
+            VMEM((2 * rows, fold.shape[2]), jnp.float32),
+            VMEM((2 * rows, w_ada.shape[1] // 2), bf),
+            VMEM((2 * rows, w_qkv.shape[1] // 2), bf),
+            VMEM((2 * rows, w_out.shape[1] // 2), bf),
+            DMA, DMA, DMA((3, 31)), DMA((3, 16)), DMA((3, 16)),
+            DMA((7,)), DMA((8,)), DMA((8,)), DMA((8,)), DMA((15,)), DMA((16,)), DMA((2,)), DMA((7,)), DMA((2,)), DMA((2,)),
+        ],
+        compiler_params=pltpu.CompilerParams(collective_id=1, has_side_effects=True, vmem_limit_bytes=32 << 20),
+        name="weights",
+    )(fold, e_fc1, e_fc2, f1, w_fc2)
+    w1s = w1s[:, :, : rows // 2].reshape(2, 16, rows, slim).transpose(1, 0, 2, 3).reshape(model, slim)
+    return ada, qkv, out, w1, w1s, w2, w2s
+
+
+def tokens_kernel(mixed, grad, gates, all_mixed, all_grad, all_gates, send, recv, l_sem):
+    here = y, z, x, c = place()
+    meet(cross_partners(here))
+    own, gathers = [], []
+    for i, (block, full, y_first) in enumerate(((mixed, all_mixed, True), (grad, all_grad, False), (gates, all_gates, True))):
+        slot = functools.partial(lambda full, n: full.at[n], full)
+        gathers.append(Gather(here, y_first, block, slot, send.at[i], recv.at[i]))
+        copy = pltpu.make_async_copy(block, slot(chip(y, z, x)), l_sem.at[i])
+        copy.start()
+        own.append(copy)
+    gather_all(gathers)
+    for copy in own:
+        copy.wait()
+
+
+def gather_tokens(mixed, grad, gates):
+    return pl.pallas_call(
+        tokens_kernel,
+        out_shape=[jax.ShapeDtypeStruct((16,) + a.shape, a.dtype) for a in (mixed, grad, gates)],
+        in_specs=[pl.BlockSpec(memory_space=VMEM)] * 3,
+        out_specs=[pl.BlockSpec(memory_space=ANY)] * 3,
+        scratch_shapes=[DMA((3, 15)), DMA((3, 16)), DMA((3,))],
+        compiler_params=pltpu.CompilerParams(collective_id=2, has_side_effects=True, vmem_limit_bytes=16 << 20),
+        name="tokens",
+    )(mixed, grad, gates)
+
+
+def nt(a, b):
+    return lax.dot_general(a, b, (((1,), (1,)), ((), ())), preferred_element_type=jnp.float32)
+
+
+def tn(a, b):
+    return lax.dot_general(a, b, (((0,), (0,)), ((), ())), preferred_element_type=jnp.float32)
+
+
+def nn(a, b):
+    return jnp.dot(a, b, preferred_element_type=jnp.float32)
+
+
+def gelu_both(h):
+    root = math.sqrt(2.0 / math.pi)
+    square = h * h
+    t = jnp.tanh(h * (root + (root * 0.044715) * square))
+    half = 0.5 * (1.0 + t)
+    slope = half + (0.5 * h) * (1.0 - t * t) * (root + (3.0 * root * 0.044715) * square)
+    return h * half, slope
+
+
+def ffn_tile(lo, shards, X, G, gates, w1, w1s, w2, w2s, act, pre, act_s, pre_s, branch, back, gc):
+    rows = pl.ds(pl.multiple_of(lo * 128, 128), shards * 128)
+    experts = w1.shape[0]
+    xt, gt = X[rows, :], G[rows, :]
+    first = lax.axis_index("gx") * experts
+    kind = lax.broadcasted_iota(jnp.int32, (16, experts * 128), 0)
+    lane = lax.broadcasted_iota(jnp.int32, (16, experts * 128), 1) // 128 + first
+    spread = ((kind == lane) | (kind == lane + 8)).astype(jnp.bfloat16)
+    gate = jnp.concatenate([tn(gates[lo + s], spread) for s in range(shards)], axis=0)
+    h = nn(xt, w1s[...])
+    a, d = gelu_both(h)
+    gi = nt(gt, w2s[...])
+    a = a.astype(jnp.bfloat16)
+    p = (gi * d).astype(jnp.bfloat16)
+    act_s[rows, :] = a
+    pre_s[rows, :] = p
+    total = nn(a, w2s[...])
+    total_back = nt(p, w1s[...])
+    sums = [jnp.zeros((8, 128), jnp.float32) for _ in range(shards)]
+    for e in range(experts):
+        h = nn(xt, w1[e])
+        a, d = gelu_both(h)
+        gi = nt(gt, w2[e])
+        g = gate[:, e * 128 : (e + 1) * 128]
+        g = jnp.concatenate([g] * (w1.shape[2] // 128), axis=1)
+        product = (a * gi).astype(jnp.bfloat16)
+        row = (lax.broadcasted_iota(jnp.int32, (8, w1.shape[2]), 0) == first + e).astype(jnp.bfloat16)
+        sums = [s + nt(row, product[i * 128 : (i + 1) * 128]) for i, s in enumerate(sums)]
+        a = (a * g).astype(jnp.bfloat16)
+        p = (gi * d * g).astype(jnp.bfloat16)
+        act[e, rows, :] = a
+        pre[e, rows, :] = p
+        total += nn(a, w2[e])
+        total_back += nt(p, w1[e])
+    branch[rows, :] = total.astype(jnp.bfloat16)
+    back[rows, :] = total_back.astype(jnp.bfloat16)
+    for s in range(shards):
+        gc[lo + s] = sums[s]
+
+
+def ffn_kernel(X, G, gates, w1, w1s, w2, w2s, branch, back, gc, d1, d1s, d2, d2s, act, pre, act_s, pre_s):
+    def body(i, carry):
+        ffn_tile(2 * i, 2, X, G, gates, w1, w1s, w2, w2s, act, pre, act_s, pre_s, branch, back, gc)
+        return carry
+
+    lax.fori_loop(0, X.shape[0] // 256, body, 0)
+
+    def grads(e, carry):
+        d1[e] = tn(X[...], pre[e]).astype(jnp.bfloat16)
+        d2[e] = tn(act[e], G[...]).astype(jnp.bfloat16)
+        return carry
+
+    lax.fori_loop(0, w1.shape[0], grads, 0)
+    d1s[...] = tn(X[...], pre_s[...])
+    d2s[...] = tn(act_s[...], G[...]).astype(jnp.bfloat16)
+
+
+def ffn(X, G, gates, w1, w1s, w2, w2s):
+    toks, model = X.shape
+    experts, _, wide = w1.shape
+    slim = w1s.shape[1]
+    bf = jnp.bfloat16
+    shape = jax.ShapeDtypeStruct
+    return pl.pallas_call(
+        ffn_kernel,
+        out_shape=[
+            shape((toks, model), bf),
+            shape((toks, model), bf),
+            shape((toks // 128, 8, 128), jnp.float32),
+            shape((experts, model, wide), bf),
+            shape((model, slim), jnp.float32),
+            shape((experts, wide, model), bf),
+            shape((slim, model), bf),
+        ],
+        in_specs=[pl.BlockSpec(memory_space=VMEM)] * 7,
+        out_specs=[pl.BlockSpec(memory_space=VMEM)] * 7,
+        scratch_shapes=[VMEM((experts, toks, wide), bf), VMEM((experts, toks, wide), bf), VMEM((toks, slim), bf), VMEM((toks, slim), bf)],
+        compiler_params=pltpu.CompilerParams(vmem_limit_bytes=56 << 20),
+        name="ffn",
+    )(X, G, gates, w1, w1s, w2, w2s)
+
+
+def sums_kernel(
+    branch, back, gc, d1, d1s, d2, d2s, sum_branch, sum_back, sum_gc, own1, own1s, own2, own2s,
+    p_branch, p_back, p_gc, r_branch, r_back, r_gc, from1, from1s, from2, from2s, out1,out1s,
+    l_sem, send, recv, t_send, t_recv, a_send, a_recv, b_send, b_recv,
+):
+    here = y, z, x, c = place()
+    me, k = chip(y, z, x), 2 * z + x
+    others = [(dy, dz, dx) for dy in (0, 1) for dz in (0, 1, 2, 3) for dx in (0, 1) if (dy, dz, dx) != (0, 0, 0)]
+    plane = [o for o in others if o[0] == 0]
+    spot = lambda dy, dz, dx: (1 - y if dy else y, (z + dz) % 4, 1 - x if dx else x)
+    sibling = device(y, z, x, 1 - c)
+    local = [
+        pltpu.make_async_copy(branch, p_branch, l_sem.at[0]),
+        pltpu.make_async_copy(back, p_back, l_sem.at[1]),
+        pltpu.make_async_copy(gc, p_gc, l_sem.at[2]),
+    ]
+    for copy in local:
+        copy.start()
+    meet([device(*spot(*o), c) for o in others] + [sibling])
+    rows1, rows1s, rows2, rows2s = from1.shape[2], from1s.shape[1], own2.shape[1], own2s.shape[0]
+    started = []
+    for n in range(8):
+        copy = remote(
+            d1.at[:, pl.ds(pl.multiple_of(rows1 * (2 * n + 1 - c), 16), rows1), :], from1.at[:, n], t_send.at[n], t_recv.at[n], sibling
+        )
+        copy.start()
+        started.append(copy)
+    for n in range(16):
+        copy = remote(
+            d1s.at[pl.ds(pl.multiple_of(rows1s * (2 * n + 1 - c), 8), rows1s), :], from1s.at[n], t_send.at[8 + n], t_recv.at[8 + n], sibling
+        )
+        copy.start()
+        started.append(copy)
+    copy = remote(d2.at[:, pl.ds(pl.multiple_of(rows2 * (1 - c), 16), rows2), :], from2, t_send.at[24], t_recv.at[24], sibling)
+    copy.start()
+    started.append(copy)
+    copy = remote(d2s.at[pl.ds(pl.multiple_of(rows2s * (1 - c), 16), rows2s), :], from2s, t_send.at[25], t_recv.at[25], sibling)
+    copy.start()
+    started.append(copy)
+
+    for copy in local:
+        copy.wait()
+    scatters = []
+    for i, (part, got, y_first) in enumerate(((p_branch, r_branch, False), (p_back, r_back, True), (p_gc, r_gc, False))):
+        take = functools.partial(lambda ref, n: ref.at[n], part)
+        land = functools.partial(lambda ref, n: ref.at[n], got)
+        scatters.append(Scatter(here, y_first, take, land, send.at[i], recv.at[i]))
+
+    order = [(0, 0, 0)] + plane
+    wide = d1.shape[2]
+    for i, o in enumerate(order):
+        ty, tz, tx = spot(*o)
+        n = 2 * tz + tx
+        remote(from1.at[:, n], from1.at[:, n], t_send.at[0], t_recv.at[n], sibling).wait_recv()
+        mine = d1[:, pl.ds(pl.multiple_of(rows1 * (2 * n + c), 16), rows1), :]
+        out1[:, n] = (mine.astype(jnp.float32) + from1[:, n].astype(jnp.float32)).astype(jnp.bfloat16)
+        target = own1.at[:, :, pl.ds(pl.multiple_of(wide * k, 128), wide)]
+        if i:
+            copy = remote(out1.at[:, n], target, a_send.at[i], a_recv.at[k], device(ty, tz, tx, c))
+            copy.start()
+            started.append(copy)
+        else:
+            keep = pltpu.make_async_copy(out1.at[:, n], target, l_sem.at[3])
+            keep.start()
+    for i, o in enumerate([(0, 0, 0)] + others):
+        spot_o = spot(*o)
+        n = chip(*spot_o)
+        remote(from1s.at[n], from1s.at[n], t_send.at[0], t_recv.at[8 + n], sibling).wait_recv()
+        out1s[n] = d1s[pl.ds(pl.multiple_of(rows1s * (2 * n + c), 8), rows1s), :] + from1s[n]
+        if i:
+            copy = remote(out1s.at[n], own1s.at[me], b_send.at[i], b_recv.at[me], device(*spot_o, c))
+            copy.start()
+            started.append(copy)
+        else:
+            keep_s = pltpu.make_async_copy(out1s.at[n], own1s.at[me], l_sem.at[4])
+            keep_s.start()
+    scatter_all(scatters)
+    remote(from2, from2, t_send.at[0], t_recv.at[24], sibling).wait_recv()
+    remote(from2s, from2s, t_send.at[0], t_recv.at[25], sibling).wait_recv()
+    own2[...] = d2[:, pl.ds(pl.multiple_of(rows2 * c, 16), rows2), :].astype(jnp.float32) + from2[...].astype(jnp.float32)
+    own2s[...] = d2s[pl.ds(pl.multiple_of(rows2s * c, 16), rows2s), :].astype(jnp.float32) + from2s[...].astype(jnp.float32)
+    sum_branch[...] = scatters[0].total()
+    sum_back[...] = scatters[1].total()
+    sum_gc[...] = scatters[2].total()
+    for scatter in scatters:
+        scatter.finish()
+    for o in plane:
+        ty, tz, tx = spot(*o)
+        n = 2 * tz + tx
+        block = own1.at[:, :, pl.ds(pl.multiple_of(wide * n, 128), wide)]
+        remote(block, block, a_send.at[0], a_recv.at[n], sibling).wait_recv()
+    for o in others:
+        n = chip(*spot(*o))
+        remote(own1s.at[n], own1s.at[n], b_send.at[0], b_recv.at[n], sibling).wait_recv()
+    keep.wait()
+    keep_s.wait()
+    for copy in started:
+        copy.wait_send()
+
+
+def scatter_sums(branch, back, gc, d1, d1s, d2, d2s):
+    bf, f32 = jnp.bfloat16, jnp.float32
+    model = branch.shape[1]
+    slim = d1s.shape[1]
+    d1s = jnp.pad(d1s, ((0, 0), (0, -slim % 128)))
+    branch, back = branch.reshape(16, -1, model), back.reshape(16, -1, model)
+    toks = branch.shape[1]
+    experts, _, wide = d1.shape
+    rows = model // 32
+    rows2, rows2s = d2.shape[1] // 2, d2s.shape[0] // 2
+    shape = jax.ShapeDtypeStruct
+    return pl.pallas_call(
+        sums_kernel,
+        out_shape=[
+            shape((toks, model), f32),
+            shape((toks, model), f32),
+            shape((8, 128), f32),
+            shape((experts, 2 * rows, 8 * wide), bf),
+            shape((16, rows, d1s.shape[1]), f32),
+            shape((experts, rows2, model), f32),
+            shape((rows2s, model), f32),
+        ],
+        in_specs=[pl.BlockSpec(memory_space=ANY)] * 3 + [pl.BlockSpec(memory_space=VMEM)] * 4,
+        out_specs=[pl.BlockSpec(memory_space=VMEM)] * 3
+        + [pl.BlockSpec(memory_space=ANY)] * 2
+        + [pl.BlockSpec(memory_space=VMEM)] * 2,
+        scratch_shapes=[
+            VMEM(branch.shape, bf), VMEM(branch.shape, bf), VMEM(gc.shape, f32),
+            VMEM((15, toks, model), bf), VMEM((15, toks, model), bf), VMEM((15, 8, 128), f32),
+            VMEM((experts, 8, 2 * rows, wide), bf), VMEM((16, rows, d1s.shape[1]), f32),
+            VMEM((experts, rows2, model), bf), VMEM((rows2s, model), bf),
+            VMEM((experts, 8, 2 * rows, wide), bf), VMEM((16, rows, d1s.shape[1]), f32),
+            DMA((5,)), DMA((3, 15)), DMA((3, 15)), DMA((26,)), DMA((26,)), DMA((8,)), DMA((8,)), DMA((16,)), DMA((16,)),
+        ],
+        compiler_params=pltpu.CompilerParams(collective_id=3, has_side_effects=True, vmem_limit_bytes=56 << 20),
+        name="sums",
+    )(branch, back, gc, d1, d1s, d2, d2s)
+
+
+def owners_kernel(
+    qkv, out, mod, total, all_mod, got_q, got_o, part, got, fin, block_sem_s, block_sem_r, send, recv, g_send, g_recv, g_pair, f_send, f_recv, l_sem,
+):
+    here = y, z, x, c = place()
+    me = chip(y, z, x)
+    sibling = device(y, z, x, 1 - c)
+    meet(cross_partners(here) + [sibling])
+    swaps = [
+        remote(qkv.at[1 - c], got_q, block_sem_s.at[0], block_sem_r.at[0], sibling),
+        remote(out.at[1 - c], got_o, block_sem_s.at[1], block_sem_r.at[1], sibling),
+    ]
+    for copy in swaps:
+        copy.start()
+    slot = lambda n: all_mod.at[n, c]
+    spread = Gather(here, True, mod, slot, g_send, g_recv, g_pair)
+    keep = pltpu.make_async_copy(mod, slot(me), l_sem.at[0])
+    keep.start()
+    spread.start()
+    for copy in swaps:
+        copy.wait()
+    rows = part.shape[2]
+    cut = part.shape[3]
+    wide = got_q.shape[1]
+    for n in range(16):
+        at = slice(n * rows, (n + 1) * rows)
+        q = (qkv[c, at, :].astype(jnp.float32) + got_q[at, :].astype(jnp.float32)).astype(jnp.bfloat16)
+        o = (out[c, at, :].astype(jnp.float32) + got_o[at, :].astype(jnp.float32)).astype(jnp.bfloat16)
+        part[0, n] = q[:, :cut]
+        part[1, n] = jnp.concatenate([q[:, cut:], o], axis=1)
+    scatters = []
+    for i, y_first in enumerate((False, True)):
+        take = functools.partial(lambda i, n: part.at[i, n], i)
+        land = functools.partial(lambda i, n: got.at[i, n], i)
+        scatters.append(Scatter(here, y_first, take, land, send.at[i], recv.at[i]))
+    scatter_all(scatters)
+    spread.second(0)
+    for step in LINE:
+        spread.line(step)
+        spread.second(step)
+    for step in (0,) + LINE:
+        spread.third(step)
+    fin[c] = jnp.concatenate([scatters[0].total(), scatters[1].total()], axis=1)
+    half = rows // 2
+    mine = pl.ds(pl.multiple_of(half * c, 8), half)
+    theirs = pl.ds(pl.multiple_of(half * (1 - c), 8), half)
+    swap = remote(fin.at[c, theirs, :], fin.at[c, theirs, :], f_send, f_recv, sibling)
+    swap.start()
+    for scatter in scatters:
+        scatter.finish()
+    spread.finish()
+    keep.wait()
+    swap.wait_send()
+    remote(fin.at[1 - c, mine, :], fin.at[1 - c, mine, :], f_send, f_recv, sibling).wait_recv()
+    total[0] = fin[0, mine, :]
+    total[1] = fin[1, mine, :]
+
+
+def to_owners(qkv, out, mod):
+    bf, f32 = jnp.bfloat16, jnp.float32
+    model = qkv.shape[1]
+    rows = model // 16
+    wide = qkv.shape[2] + out.shape[2]
+    cut = wide // 2
+    shape = jax.ShapeDtypeStruct
+    return pl.pallas_call(
+        owners_kernel,
+        out_shape=[shape((2, rows // 2, wide), f32), shape((16, 2) + mod.shape, bf)],
+        in_specs=[pl.BlockSpec(memory_space=VMEM)] * 3,
+        out_specs=[pl.BlockSpec(memory_space=VMEM), pl.BlockSpec(memory_space=ANY)],
+        scratch_shapes=[
+            VMEM(qkv.shape[1:], bf), VMEM(out.shape[1:], bf), VMEM((2, 16, rows, cut), bf), VMEM((2, 15, rows, cut), bf),
+            VMEM((2, rows, wide), f32),
+            DMA((2,)), DMA((2,)), DMA((2, 15)), DMA((2, 15)), DMA((31,)), DMA((16,)), DMA((16,)), DMA, DMA, DMA((1,)),
+        ],
+        compiler_params=pltpu.CompilerParams(collective_id=4, has_side_effects=True, vmem_limit_bytes=40 << 20),
+        name="owners",
+    )(qkv, out, mod)
 
 
 def layer_norm(values):
@@ -60,7 +745,117 @@
     return jnp.einsum("tf,df->td", left_side, right_side, preferred_element_type=jnp.float32)
 
 
-def on_device(
+def dot_halves(left_side, halves):
+    return jnp.concatenate([dot_float(left_side, halves[0]), dot_float(left_side, halves[1])], axis=1)
+
+
+def by_slices(
+    tokens, timesteps, lengths, routes, cotangent, w_ada, w_qkv, w_out, w_fc1, w_fc2, w_router, e_fc1, e_fc2
+):
+    tok_count, model_width = tokens.shape
+    head_count = HEADS
+    head_size = model_width // head_count
+    expert_count = w_router.shape[1]
+    score_scale = head_size ** (-0.5)
+    residual = tokens.astype(jnp.float32)
+    member, item_of = membership(lengths[0], tok_count)
+    ada, qkv_w, out_w, w1, w1s, w2, w2s = gather_weights(w_ada, w_qkv, w_out, w_fc1, w_fc2, e_fc1, e_fc2)
+    router_full = lax.all_gather(w_router, ("gx", "gy"), axis=0, tiled=True)
+    condition = jax.nn.silu(sinusoid(timesteps, model_width)).astype(jnp.bfloat16)
+    modulation = dot_halves(condition, ada)
+    token_mod = jnp.dot(member, modulation, precision=precise)
+    shift_attn, scale_attn, gate_attn, shift_mlp, scale_mlp, gate_mlp = jnp.split(token_mod, 6, axis=1)
+    attn_in = modulate(residual, shift_attn, scale_attn).astype(jnp.bfloat16)
+    qkv_low = dot_halves(attn_in, qkv_w).astype(jnp.bfloat16)
+    queries, key_rows, value_rows = [
+        portion.reshape(tok_count, head_count, head_size) for portion in jnp.split(qkv_low, 3, axis=1)
+    ]
+    same_item = item_of[:, None] == item_of[None, :]
+    scores = (
+        jnp.einsum("qhd,khd->hqk", queries, key_rows, preferred_element_type=jnp.float32) * score_scale
+    )
+    scores = jnp.where(same_item[None], scores, -1e30)
+    attn_probs = jax.nn.softmax(scores, axis=-1)
+    probs_low = attn_probs.astype(jnp.bfloat16)
+    attn_low = jnp.einsum("hqk,khd->qhd", probs_low, value_rows, preferred_element_type=jnp.float32)
+    attn_low = attn_low.reshape(tok_count, model_width).astype(jnp.bfloat16)
+    attn_proj = dot_halves(attn_low, out_w)
+    middle = residual + gate_attn * attn_proj
+    mixed_in = modulate(middle, shift_mlp, scale_mlp).astype(jnp.bfloat16)
+    out_grad = cotangent.astype(jnp.float32)
+    grad_branch = out_grad * gate_mlp
+    chance = jax.nn.softmax(dot_float(mixed_in, router_full), axis=-1)
+    expert_ids = jnp.arange(expert_count, dtype=jnp.int32)
+    chosen = jnp.sum((routes[:, :, None] == expert_ids[None, None, :]).astype(jnp.float32), axis=1)
+    gates = (chosen * chance).T
+    gates_high = gates.astype(jnp.bfloat16)
+    gates_low = (gates - gates_high.astype(jnp.float32)).astype(jnp.bfloat16)
+    all_mixed, all_grad, all_gates = gather_tokens(
+        mixed_in, grad_branch.astype(jnp.bfloat16), jnp.concatenate([gates_high, gates_low], axis=0)
+    )
+    flat = lambda a: a.reshape(-1, model_width)
+    parts = ffn(flat(all_mixed), flat(all_grad), all_gates, w1, w1s, w2, w2s)
+    branch, grad_mixed, grad_chance, own1, own1s, sum_e_out, sum_fc2 = scatter_sums(*parts)
+    sum_e_in = own1.astype(jnp.float32)
+    slim = w1s.shape[1]
+    sum_fc1 = own1s[:, :, :slim].transpose(1, 0, 2).reshape(w_fc1.shape)
+    output = (middle + gate_mlp * branch).astype(jnp.bfloat16)
+    grad_gate_mlp = out_grad * branch
+    grad_chance = grad_chance.T * chosen
+    grad_logits = chance * (grad_chance - jnp.sum(grad_chance * chance, axis=-1, keepdims=True))
+    grad_logits = grad_logits.astype(jnp.bfloat16)
+    term_router = dot_rows(mixed_in, grad_logits)
+    sum_router = lax.psum_scatter(term_router, ("gx", "gy"), scatter_dimension=0, tiled=True)
+    grad_mixed = grad_mixed + dot_cols(grad_logits, router_full)
+    unused_mix, mix_back = jax.vjp(modulate, middle, shift_mlp, scale_mlp)
+    grad_mid_norm, grad_shift_mlp, grad_scale_mlp = mix_back(grad_mixed)
+    grad_middle = out_grad + grad_mid_norm
+    grad_gate_attn = grad_middle * attn_proj
+    grad_proj = (grad_middle * gate_attn).astype(jnp.bfloat16)
+    half = model_width // 2
+    term_out = jnp.stack([dot_rows(attn_low, grad_proj[:, c * half : (c + 1) * half]) for c in (0, 1)])
+    grad_attn = sum(dot_cols(grad_proj[:, c * half : (c + 1) * half], out_w[c]) for c in (0, 1))
+    grad_attn = grad_attn.astype(jnp.bfloat16).reshape(tok_count, head_count, head_size)
+    grad_probs = jnp.einsum("qhd,khd->hqk", grad_attn, value_rows, preferred_element_type=jnp.float32)
+    grad_values = jnp.einsum("hqk,qhd->khd", probs_low, grad_attn, preferred_element_type=jnp.float32)
+    grad_scores = attn_probs * (grad_probs - jnp.sum(grad_probs * attn_probs, axis=-1, keepdims=True))
+    grad_scores = grad_scores.astype(jnp.bfloat16)
+    grad_queries = (
+        jnp.einsum("hqk,khd->qhd", grad_scores, key_rows, preferred_element_type=jnp.float32) * score_scale
+    )
+    grad_keys = (
+        jnp.einsum("hqk,qhd->khd", grad_scores, queries, preferred_element_type=jnp.float32) * score_scale
+    )
+    grad_qkv = jnp.concatenate(
+        [g.reshape(tok_count, model_width) for g in (grad_queries, grad_keys, grad_values)], axis=1
+    ).astype(jnp.bfloat16)
+    half = grad_qkv.shape[1] // 2
+    term_qkv = jnp.stack([dot_rows(attn_in, grad_qkv[:, c * half : (c + 1) * half]) for c in (0, 1)])
+    grad_attn_in = sum(dot_cols(grad_qkv[:, c * half : (c + 1) * half], qkv_w[c]) for c in (0, 1))
+    unused_pre, pre_back = jax.vjp(modulate, residual, shift_attn, scale_attn)
+    grad_input_norm, grad_shift_attn, grad_scale_attn = pre_back(grad_attn_in)
+    d_tokens = grad_middle + grad_input_norm
+    grad_token_mod = jnp.concatenate(
+        [grad_shift_attn, grad_scale_attn, grad_gate_attn, grad_shift_mlp, grad_scale_mlp, grad_gate_mlp], axis=1
+    )
+    grad_modulation = jnp.einsum("ti,tc->ic", member, grad_token_mod, precision=precise).astype(jnp.bfloat16)
+    items = grad_modulation.shape[0]
+    both = jnp.concatenate([grad_modulation, condition], axis=1)
+    width = both.shape[1]
+    tile = jnp.pad(both.reshape(items * 8, width // 8), ((0, 0), (0, -(width // 8) % 128)))
+    total, all_tile = to_owners(term_qkv.astype(jnp.bfloat16), term_out.astype(jnp.bfloat16), tile)
+    all_both = all_tile[..., : width // 8].reshape(-1, width)
+    all_modgrad, all_condition = all_both[:, : grad_modulation.shape[1]], all_both[:, grad_modulation.shape[1] :]
+    own_share = w_ada.shape[0]
+    own_start = lax.axis_index(("gx", "gy")) * own_share
+    own_condition = lax.dynamic_slice_in_dim(all_condition, own_start, own_share, 1)
+    owned_ada = dot_rows(own_condition, all_modgrad)
+    sum_qkv = jnp.concatenate([total[0, :, :half], total[1, :, :half]], axis=1)
+    sum_out = jnp.concatenate([total[0, :, half:], total[1, :, half:]], axis=1)
+    return (output, d_tokens, owned_ada, sum_qkv, sum_out, sum_fc1, sum_fc2, sum_router, sum_e_in, sum_e_out)
+
+
+def by_weights(
     tokens,
     timesteps,
     lengths,
@@ -343,6 +1138,7 @@
         P("gx", "gy", None),
         P("gx", "gy", None),
     )
+    step = by_slices if dict(mesh.shape) == {"gx": 2, "gy": 16} else by_weights
     return jax.shard_map(
-        on_device, mesh=mesh, in_specs=in_specs, out_specs=out_specs, check_vma=False
-    )
+        step, mesh=mesh, in_specs=in_specs, out_specs=out_specs, check_vma=False
+    )

time: 1430 us -> 492 us (0.34)
  waiting for transfers between devices: 1060 us -> 0 us
  Pallas kernels: 0 us -> 339 us
  matrix products: 128 us -> 17.9 us
  blocking collectives: 153 us -> 95.8 us
  starting transfers between devices: 16.3 us -> 0 us
  between operations: 16.5 us -> 1.69 us
    reduce_scatter x10 -> x0, waiting for transfers between devices: 614 us -> none  [the longest x1 197 us: on_device(): lax.psum_scatter(term_e_in.astype(jnp.bfloat16), 'gy', scatter_dimension=...]
    all_gather x7 -> x0, waiting for transfers between devices: 404 us -> none  [the longest x1 89.2 us: on_device(): lax.all_gather(e_fc1, 'gy', axis=1, tiled=True)]
    pallas_call x0 -> x5, Pallas kernels: none -> 339 us  [the longest x1 96.5 us: scatter_sums(): pl.pallas_call(sums_kernel, out_shape=[shape((toks, model), f32), shape((...]
    dot_general x15 -> x7, matrix products: 81.5 us -> 6.23 us  [the longest x1 1.67 us: by_slices(): jnp.einsum('hqk,qhd->khd', probs_low, grad_attn, preferred_element_type=j...]
    all_gather x3 -> x1, blocking collectives: 122 us -> 56.7 us  [by_slices(): router_full = lax.all_gather(w_router, ('gx', 'gy'), axis=0, tiled=True)]
    all_to_all x4 -> x0, waiting for transfers between devices: 41.1 us -> none  [the longest x1 17.2 us: on_device(): lax.all_to_all(result, 'gx', split_axis=1, concat_axis=0, tiled=True)]
    all_to_all x4 -> x0, starting transfers between devices: 15.2 us -> none  [the longest x1 4.36 us: on_device(): lax.all_to_all(slot_rows, 'gx', split_axis=0, concat_axis=1, tiled=True)]
  transfers between devices with their start and end apart: 22 -> 0, of which waited for: 18 -> 0; matrix products, arithmetic and copies ran while one was open for 12% -> 0% of each run, Pallas kernels for 0% -> 0%
where the time goes in v1:
time: 492 us; the launch traced here: 491 us
  Pallas kernels  339 us (69%)
  blocking collectives  95.8 us (19%)
  local copies, waits for them, and re-layouts  24.3 us (5%)
  matrix products  17.9 us (4%)
  other arithmetic  12.7 us (3%)
    pallas_call x1, Pallas kernels, scatter_sums(): pl.pallas_call(sums_kernel, out_shape=[shape((toks, model), f32), shape((...  96.5 us
    pallas_call x1, Pallas kernels, gather_weights(): pl.pallas_call(weights_kernel, out_shape=out_shape, in_specs=[pl.BlockSpe...  84.3 us
    pallas_call x1, Pallas kernels, ffn(): pl.pallas_call(ffn_kernel, out_shape=[shape((toks, model), bf), shape((to...  57.7 us
    pallas_call x1, Pallas kernels, gather_tokens(): pl.pallas_call(tokens_kernel, out_shape=[jax.ShapeDtypeStruct((16,) + a.s...  56.9 us
    all_gather x1, blocking collectives, by_slices(): router_full = lax.all_gather(w_router, ('gx', 'gy'), axis=0, tiled=True)  56.7 us
    pallas_call x1, Pallas kernels, to_owners(): pl.pallas_call(owners_kernel, out_shape=[shape((2, rows // 2, wide), f32)...  43.1 us
    unnamed x1, blocking collectives  39.1 us
    unnamed x115, local copies, waits for them, and re-layouts  13.8 us

profile of v1, /device:TPU:0, one launch (start us, length us, event | category | flops | bytes accessed | tf_op | source)
XLA Modules:
  0.0 491.0 jit_solution(16373066703954394420)
XLA Ops:
  4.0 1.3 copy-done.5
  6.2 84.3 %weights.1 = (bf16[2,768,2304]{2,1,0:T(8,128)(2,1)S(1)}, bf16[2,768,1152]{2,1,0:T(8,128)(2,1)S(1)}, bf16[2,768,384]{2,1,0:T(8,128)(2,1)S(1)}, bf16[4,768,384]{2,...) custom-call(f32[2,24,3840]{2,1,0:T(8,128)S(1)} %maximum_convert_fusi, ...), custom_call_target="tpu_custom_call" | custom-call | tf_op jit(solution)/shard_map/weights/pallas_call | solution.py:333
  90.5 1.8 copy-done.6
  94.7 1.1 fusion.65
  98.1 1.3 fusion.93
  100.9 1.5 fusion.89
  102.8 56.7 %all-gather = bf16[32,24,8]{1,2,0:T(8,128)(2,1)S(1)} all-gather(bf16[1,24,8]{1,2,0:T(8,128)(2,1)S(1)} %bitcast.166), channel_id=1, replica_groups=mesh['gx'=2,'gy'=16] {'gx','gy'}, dimensions={0}, use_global_device_ids=true | all-gather | bytes 12672 | tf_op jit(solution)/shard_map/all_gather | solution.py:763
  160.0 56.9 %tokens.1 = (bf16[16,128,768]{2,1,0:T(8,128)(2,1)S(1)}, bf16[16,128,768]{2,1,0:T(8,128)(2,1)S(1)}, bf16[16,16,128]{2,1,0:T(8,128)(2,1)S(1)}) custom-call(bf16[128,768]{1,0:T(8,128)(2,1)S(1)} %get-tuple-element.70.mixed, bf16[128,768]{1,0:T(8,128)(2,1)S(1)} %get-tuple-element.69.grad, bf16[16,128]{1,0:T(8,128)(2,1)S(1)} %pad_maximum_fusion.14.gates), custom_call_target="tpu_custom_call" | custom-call | tf_op jit(solution)/shard_map/tokens/pallas_call | solution.py:369
  216.9 1.7 copy-done
  218.6 1.6 copy-done.1
  221.9 57.7 %ffn.1 = (bf16[2048,768]{1,0:T(8,128)(2,1)}, bf16[2048,768]{1,0:T(8,128)(2,1)}, f32[16,8,128]{2,1,0:T(8,128)}, bf16[4,768,384]{2,1,0:T(8,128)(2,1)}, f32[768,192...) custom-call(bf16[2048,768]{1,0:T(8,128)(2,1)} %bitcast.133, bf16[2048,768]{1,0:T(8,128)(2,1)} %bitcast.134, ...), custom_call_target="tpu_custom_call" | custom-call | tf_op jit(solution)/shard_map/ffn/pallas_call | solution.py:464
  279.6 2.1 pad.13.d1s
  281.7 96.5 %sums.1 = (f32[128,768]{1,0:T(8,128)}, f32[128,768]{1,0:T(8,128)}, f32[8,128]{1,0:T(8,128)}, bf16[4,48,3072]{2,1,0:T(8,128)(2,1)}, f32[16,24,256]{2,1,0:T(8,128)...) custom-call(bf16[16,128,768]{2,1,0:T(8,128)(2,1)} %bitcast.141, bf16[16,128,768]{2,1,0:T(8,128)(2,1)} %bitcast.142, ...), custom_call_target="tpu_custom_call" | custom-call | tf_op jit(solution)/shard_map/sums/pallas_call | solution.py:594
  379.7 1.4 multiply_reduce_fusion.1
  381.1 1.8 fusion.88
  384.9 1.7 convolution_convert_fusion.7
  386.6 1.3 multiply_reduce_fusion
  388.7 1.2 copy-done.8
  390.7 1.8 constant_dynamic-update-slice_fusion.1
  392.5 1.3 fusion.87
  398.9 43.1 %owners.1 = (f32[2,24,1536]{2,1,0:T(8,128)S(1)}, bf16[16,2,16,768]{3,2,1,0:T(8,128)(2,1)S(1)}) custom-call(bf16[2,768,1152]{2,1,0:T(8,128)(2,1)S(1)} %pad_maximum_fusion.qkv, bf16[2,768,384]{2,1,0:T(8,128)(2,1)S(1)} %pad_maximum_fusion.1.out, bf16[16,768]{1,0:T(8,128)(2,1)S(1)} %pad.14.mod), custom_call_target="tpu_custom_call" | custom-call | tf_op jit(solution)/shard_map/owners/pallas_call | solution.py:686
  445.4 39.1 %all-reduce.3 = f32[768,8]{0,1:T(8,128)S(1)} all-reduce(f32[768,8]{0,1:T(8,128)S(1)} %fusion.95), channel_id=2, replica_groups=mesh['gx'=2,'gy'=16] {'gx','gy'}, use_global_device_ids=true, to_apply=%region_16.17.clone | all-reduce | flops 6144 | bytes 49152
  485.1 1.7 convert_element_type.119
  489.6 1.4 copy.92
  (192 shorter events, 29.1 us)
Async XLA Ops:
  0.6 2.8 copy-start.37
  0.7 3.3 copy-start.4
  3.7 88.6 %copy-start.53 = (s32[2]{0:T(128)S(1)}, s32[2]{0:T(128)}, u32[]{:S(2)}) copy-start(s32[2]{0:T(128)} %param.14) | copy-start | bytes 28
  92.2 2.3 copy-start.9
  93.0 2.9 copy-start.15
  94.7 3.3 copy-start.41
  97.8 2.4 copy-start.29
  98.0 123.9 %copy-start.31 = (bf16[128,768]{0,1:T(8,128)(2,1)}, bf16[128,768]{0,1:T(8,128)(2,1)S(1)}, u32[]{:S(2)}) copy-start(bf16[128,768]{0,1:T(8,128)(2,1)S(1)} %copy.67) | copy-start | bytes 589828
  100.2 2.4 copy-start.16
  100.2 2.4 copy-start.13
  100.2 2.4 copy-start.18
  100.9 116.0 %copy-start.25 = (f32[128,384]{1,0:T(8,128)}, f32[128,384]{1,0:T(8,128)S(1)}, u32[]{:S(2)}) copy-start(f32[128,384]{1,0:T(8,128)S(1)} %fusion.37) | copy-start | bytes 589828
  100.9 59.0 %copy-start.50 = (s32[128,2]{0,1:T(2,128)S(1)}, s32[128,2]{0,1:T(2,128)}, u32[]{:S(2)}) copy-start(s32[128,2]{0,1:T(2,128)} %param.16) | copy-start | bytes 3076
  102.6 278.4 %copy-start.43 = (f32[128]{0:T(128)}, f32[128]{0:T(128)S(1)}, u32[]{:S(2)}) copy-start(f32[128]{0:T(128)S(1)} %fusion.79) | copy-start | bytes 1540
  281.7 98.0 %copy-start.14 = (f32[128,4608]{1,0:T(8,128)S(1)}, f32[128,4608]{1,0:T(8,128)}, u32[]{:S(2)}) copy-start(f32[128,4608]{1,0:T(8,128)} %copy-done.12) | copy-start | bytes 7077892
  378.3 4.7 copy-start.19
  384.1 2.5 copy-start.33
  384.1 2.5 copy-start.36
  390.6 3.2 copy-start.24
  390.6 3.2 copy-start.26
  390.7 3.2 copy-start.49
  392.5 2.3 copy-start.44
  442.0 43.1 %copy-start.28 = (bf16[4,48,3072]{2,1,0:T(8,128)(2,1)S(1)}, bf16[4,48,3072]{2,1,0:T(8,128)(2,1)}, u32[]{:S(2)}) copy-start(bf16[4,48,3072]{2,1,0:T(8,128)(2,1)} %get-tuple-element.60) | copy-start | bytes 3538948
  485.1 4.5 copy-start.20
  (31 other events, 46.5 us)
